TPU v7x, 32 devices: a whole 2x2x4 slice. The times are simulated.
32 devices in a mesh: dp: 2 (over x), blk: 4 (over z), head: 4 (over y, core).
Axes of the slice: x: 2, y: 2, z: 4, core: 2. Of those that a mesh axis runs over, the one named last changes fastest.
Arguments:
- tokens: bfloat16 [2, 2048, 768], P('dp', ('blk', 'head')), may hold values from -6 to 6
- order: int32 [2, 2048], P('dp', ('blk', 'head')), may hold values from 0 to 2047, each once within a row
- expert_ids: int32 [2, 2048, 1], replicated, may hold values from 0 to 7
- norm1_gain: bfloat16 [768], P(('dp', 'blk', 'head')), may hold values from 0.5 to 1.5
- w_query: bfloat16 [768, 768], P(('dp', 'blk', 'head')), may hold values from -0.3125 to 0.3125
- w_key: bfloat16 [768, 768], P(('dp', 'blk', 'head')), may hold values from -0.3125 to 0.3125
- w_value: bfloat16 [768, 768], P(('dp', 'blk', 'head')), may hold values from -0.21875 to 0.21875
- w_attn_out: bfloat16 [768, 768], P(('dp', 'blk', 'head')), may hold values from -1.25 to 1.25
- rel_table: bfloat16 [384], P(('dp', 'blk', 'head')), may hold values from -3 to 3
- norm2_gain: bfloat16 [768], P(('dp', 'blk', 'head')), may hold values from 0.5 to 1.5
- w_router: bfloat16 [768, 8], P(('dp', 'blk', 'head')), may hold values from -0.15625 to 0.15625
- w_in: bfloat16 [8, 768, 3072], P(('dp', 'blk')), may hold values from -0.21875 to 0.21875
- w_out: bfloat16 [8, 3072, 768], P(('dp', 'blk')), may hold values from -3.5 to 3.5
- cotangent: bfloat16 [2, 2048, 768], P('dp', ('blk', 'head')), may hold values from -6 to 6
Outputs:
- layer_out: bfloat16 [2, 2048, 768], P('dp', ('blk', 'head'))
- grad_tokens: bfloat16 [2, 2048, 768], P('dp', ('blk', 'head'))
- grad_norm1_gain: float32 [768], P(('dp', 'blk', 'head'))
- grad_w_query: float32 [768, 768], P(('dp', 'blk', 'head'))
- grad_w_key: float32 [768, 768], P(('dp', 'blk', 'head'))
- grad_w_value: float32 [768, 768], P(('dp', 'blk', 'head'))
- grad_w_attn_out: float32 [768, 768], P(('dp', 'blk', 'head'))
- grad_rel_table: float32 [384], P(('dp', 'blk', 'head'))
- grad_norm2_gain: float32 [768], P(('dp', 'blk', 'head'))
- grad_w_router: float32 [768, 8], P(('dp', 'blk', 'head'))
- grad_w_in: float32 [8, 768, 3072], P(('dp', 'blk'))
- grad_w_out: float32 [8, 3072, 768], P(('dp', 'blk'))
Inputs may be any that keep to these rules, and one draw needn't show every extreme that they name: `expert_ids`: every expert is named by some token. `order`: within each sequence every value appears once.
All inputs are finite; a program needn't handle non-finite values.
Results may differ from a plain program's by a relative error of at most 0.033.
Values may be sent and summed in bfloat16 or wider, within the bound.
A program may use at most 192 MiB of HBM per device.

v0:
```python
import functools
import itertools
import types

import jax
import jax.numpy as jnp
from jax import lax
from jax.experimental import pallas as pl
from jax.experimental.pallas import tpu as pltpu
from jax.sharding import PartitionSpec as P

HEAD_COUNT = 12
HEAD_SIZE = 64
BUCKETS = 32
BLOCK = 256
EPSILON = 1e-06
AUX_WEIGHT = 1.0
LIMITS = (1, 2, 3, 4, 5, 6, 7, 8, 12, 16, 23, 32, 46, 64, 91)
INV_ROOT_TWO = 0.7071067811865476
INV_ROOT_TWO_PI = 0.3989422804014327
LANES = 128
VMEM_LIMIT = 62 * 1024 * 1024
PASSED = (
    "layer_ref", "gtok_ref", "gain1_ref", "gq_ref", "gk_ref", "gv_ref", "go_ref", "table_ref",
    "gain2_ref", "router_out",
)
MESH = pl.DeviceIdType.MESH
F32 = jnp.float32
BF16 = jnp.bfloat16


def both_halves(values):
    n = values.shape[0] // 2
    return jnp.concatenate([values[:n], values[n:]], axis=1)


def line_order(b, nb):
    out = [(b, b >= 0)]
    for k in range(1, nb):
        out.append((b - k, b >= k))
        out.append((b + k, b + k < nb))
    return out


class Sends:
    def __init__(self, sems):
        self.sems, self.made = sems, []

    def put(self, src, dst, recv, device, cond=None):
        c = remote(src, dst, self.sems.at[len(self.made)], recv, device)
        self.made.append((c, cond))
        self.each(c.start, cond)

    def each(self, action, cond):
        if cond is None:
            action()
        else:
            pl.when(cond)(action)

    def finish(self):
        for c, cond in self.made:
            self.each(c.wait_send, cond)


class Sizes:
    def __init__(self, n_dp, n_blk, n_head, rows, width, experts, hidden, piece):
        self.n_dp, self.n_blk, self.n_head = n_dp, n_blk, n_head
        self.ndev = n_dp * n_blk * n_head
        self.ns = n_blk * n_head
        self.R, self.D, self.E, self.FF, self.PT = rows, width, experts, hidden, piece
        self.S = piece * self.ns
        self.nq = self.S // BLOCK
        self.hb = HEAD_COUNT // n_blk
        self.cap = (5 * piece + 4 * experts - 1) // (4 * experts)
        self.cap8 = (self.cap + 7) // 8 * 8
        self.NG = n_dp * n_blk
        self.RL = HEAD_COUNT * BUCKETS // self.ndev
        self.wide = 4 * width + LANES
        self.per = BLOCK // piece
        assert self.hb < n_head and self.hb * n_blk == HEAD_COUNT
        assert experts == self.NG and n_head == 4


    def holder(self, n):
        return n // self.hb, n % self.hb + n // self.hb % 2


def nt(a, b):
    return lax.dot_general(a, b, (((1,), (1,)), ((), ())), preferred_element_type=F32)


def tn(a, b):
    return lax.dot_general(a, b, (((0,), (0,)), ((), ())), preferred_element_type=F32)


def nn(a, b):
    return jnp.dot(a, b, preferred_element_type=F32)


def place():
    return lax.axis_index("dp"), lax.axis_index("blk"), lax.axis_index("head")


def signal(device):
    pl.semaphore_signal(
        pltpu.get_barrier_semaphore(), inc=1, device_id=device, device_id_type=MESH
    )


def await_barrier(count):
    pl.semaphore_wait(pltpu.get_barrier_semaphore(), count)


def remote(src, dst, send, recv, device):
    return pltpu.make_async_remote_copy(
        src_ref=src, dst_ref=dst, send_sem=send, recv_sem=recv, device_id=device, device_id_type=MESH
    )


def flatten_rows(blocks):
    count, rows, lanes = blocks.shape
    wide = blocks.astype(F32)
    if rows % 8 == 0:
        return wide.reshape(count * rows, lanes)
    return jnp.concatenate([wide[i] for i in range(count)], axis=0)


def split_rows(dst_ref, values, rows):
    count = values.shape[0] // rows
    if rows % 8 == 0:
        dst_ref[...] = values.reshape(count, rows, values.shape[1]).astype(dst_ref.dtype)
    else:
        for i in range(count):
            dst_ref[i] = values[i * rows : (i + 1) * rows].astype(dst_ref.dtype)


def activate(pre):
    phi, bell = normal_parts(pre)
    slope = phi + pre * bell * INV_ROOT_TWO_PI
    return (pre * phi).astype(BF16), slope.astype(BF16)


def grad_pre(grad_out, w, slope):
    hidden = nt(grad_out, w).astype(BF16).astype(F32)
    return (hidden * slope.astype(F32)).astype(BF16)


def normal_parts(v):
    bell = jnp.exp(-0.5 * v * v)
    t = 1.0 / (1.0 + (0.3275911 * INV_ROOT_TWO) * jnp.abs(v))
    poly = t * (
        0.254829592
        + t * (-0.284496736 + t * (1.421413741 + t * (-1.453152027 + t * 1.061405429)))
    )
    tail = 0.5 * poly * bell
    return jnp.where(v >= 0, 1.0 - tail, tail), bell


def bias_tile(table, shift):
    j = lax.broadcasted_iota(jnp.int32, (BLOCK, BLOCK), 0)
    i = lax.broadcasted_iota(jnp.int32, (BLOCK, BLOCK), 1)
    dist = j - i + shift
    mag = jnp.abs(dist)
    half = BUCKETS // 2
    out = jnp.broadcast_to(table[0:1, 0:1], (BLOCK, BLOCK))
    for n, limit in enumerate(LIMITS):
        low = table[n + 1 : n + 2, 0:1]
        if shift == 0:
            high = table[half + n + 1 : half + n + 2, 0:1]
            out = jnp.where(mag >= limit, jnp.where(dist > 0, high, low), out)
        else:
            out = jnp.where(mag >= limit, low, out)
    return out


def bucket_sums(tile, shift):
    row = lax.broadcasted_iota(jnp.int32, (BLOCK, BLOCK), 0)
    column = lax.broadcasted_iota(jnp.int32, (BLOCK, BLOCK), 1)
    turn = (row + column == BLOCK - 1).astype(BF16)
    high = tile.astype(BF16)
    rest = (tile - high.astype(F32)).astype(BF16)
    turned = nn(turn, high) + nn(turn, rest)
    wide = jnp.concatenate([turned, jnp.zeros((BLOCK, BLOCK), F32)], axis=1)
    skewed = pltpu.roll(wide, 0, 1, stride=1, stride_axis=0)
    line = jnp.sum(skewed.reshape(BLOCK // 8, 8, 2 * BLOCK), axis=0)
    behind = lax.broadcasted_iota(jnp.int32, (2 * BLOCK, HEAD_SIZE), 0) - (BLOCK - 1) + shift
    bucket = jnp.zeros((2 * BLOCK, HEAD_SIZE), jnp.int32)
    for limit in LIMITS:
        bucket = bucket + (jnp.abs(behind) >= limit).astype(jnp.int32)
    bucket = bucket + jnp.where(behind < 0, BUCKETS // 2, 0)
    hot = bucket == lax.broadcasted_iota(jnp.int32, (2 * BLOCK, HEAD_SIZE), 1)
    parts = jnp.dot(
        line, hot.astype(F32), precision=lax.Precision.HIGHEST, preferred_element_type=F32
    )
    return jnp.sum(parts, axis=0, keepdims=True)


class Spread:
    def __init__(self, z, src, dst, send, recv, y_first, lanes):
        self.z, self.src, self.dst, self.recv = z, src, dst, recv
        self.sends, self.lanes = Sends(send), lanes
        d, b, h = place()
        self.at = (d, b, h)
        nh, nd = z.n_head, z.n_dp
        self.hy = lax.rem(h + 2, nh)
        self.hc = h + 1 - 2 * lax.rem(h, 2)
        self.hyc = lax.rem(self.hc + 2, nh)
        dto = [lax.rem(d + k, nd) for k in range(1, nd)]
        dfrom = [lax.rem(d + nd - k, nd) for k in range(1, nd)]
        ys = ([(d, self.hy)], [(d, self.hy)])
        xs = ([(p, h) for p in dto], [(p, h) for p in dfrom])
        self.first, self.second = (ys, xs) if y_first else (xs, ys)
        if y_first:
            self.second_slots = [(p, hh) for p in dfrom for hh in (h, self.hy)]
        else:
            self.second_slots = [(p, self.hy) for p in [d] + dfrom]
        self.core_slots = [(p, hh) for p in [d] + dfrom for hh in (self.hc, self.hyc)]

    def slot(self, dd, bb, hh):
        return (dd * self.z.n_blk + bb) * self.z.n_head + hh

    def ref(self, slot):
        return self.dst.at[slot, :, self.lanes]

    def put(self, src, slot, device, cond=None):
        self.sends.put(src, self.ref(slot), self.recv.at[slot], device, cond)

    def got(self, slot):
        d, b, h = self.at
        ref = self.ref(slot)
        remote(ref, ref, self.sends.sems.at[0], self.recv.at[slot], (d, b, self.hc)).wait_recv()

    def steps(self):
        d, b, h = self.at
        nb = self.z.n_blk

        def begin():
            mine = self.slot(d, b, h)
            self.put(self.src, mine, (d, b + 1, h), b + 1 < nb)
            self.put(self.src, mine, (d, b - 1, h), b >= 1)
            for dd, hh in self.first[0] + self.second[0] + [(d, self.hc)]:
                self.put(self.src, mine, (dd, b, hh))

        def line_arrival(k):
            for f, cond, to, more in (
                (b - k, b >= k, b + 1, b + 1 < nb),
                (b + k, b + k < nb, b - 1, b >= 1),
            ):
                slot = self.slot(d, f, h)
                pl.when(cond)(functools.partial(self.got, slot))
                if k < nb - 1:
                    self.put(self.ref(slot), slot, (d, to, h), cond & more)
                for dd, hh in self.first[0] + self.second[0] + [(d, self.hc)]:
                    self.put(self.ref(slot), slot, (dd, b, hh), cond)

        def first_arrival(p, f, cond):
            slot = self.slot(p[0], f, p[1])
            pl.when(cond)(functools.partial(self.got, slot))
            for dd, hh in self.second[0] + [(d, self.hc)]:
                self.put(self.ref(slot), slot, (dd, b, hh), cond)

        def second_arrival(p, f, cond):
            slot = self.slot(p[0], f, p[1])
            pl.when(cond)(functools.partial(self.got, slot))
            self.put(self.ref(slot), slot, (d, b, self.hc), cond)

        out = [begin]
        for k in range(1, nb):
            out.append(functools.partial(line_arrival, k))
        for p in self.first[1]:
            for f, cond in line_order(b, nb):
                out.append(functools.partial(first_arrival, p, f, cond))
        for p in self.second_slots:
            for f, cond in line_order(b, nb):
                out.append(functools.partial(second_arrival, p, f, cond))
        return out

    def finish(self):
        d, b, h = self.at
        for p in self.core_slots:
            for f in range(self.z.n_blk):
                self.got(self.slot(p[0], f, p[1]))
        self.sends.finish()


def spread_copies(z, y_first):
    nb, nd = z.n_blk, z.n_dp
    peers = 1 + nd - 1 + 1
    first = 1 if y_first else nd - 1
    second = peers - 1 - first
    second_slots = 2 * (nd - 1) if y_first else nd
    line = 2 * nb - 1
    return 2 + peers + (nb - 1) * 2 * (peers + 1) + first * line * (second + 1) + second_slots * line


class Place:
    def __init__(self, z):
        self.d, self.b, self.h = d, b, h = place()
        self.s = b * z.n_head + h
        self.me = d * z.ns + self.s
        self.g = d * z.n_blk + b
        first = lax.rem(b, 2)
        self.active = (h >= first) & (h < first + z.hb)
        self.hd = b * z.hb + jnp.clip(h - first, 0, z.hb - 1)
        self.hy = lax.rem(h + 2, z.n_head)
        self.hc = h + 1 - 2 * lax.rem(h, 2)
        self.hyc = lax.rem(self.hc + 2, z.n_head)
        self.z = z

    def any_peer(self, k):
        z = self.z
        t = lax.rem(self.me + k, z.ndev)
        return t, (t // z.ns, lax.rem(t // z.n_head, z.n_blk), lax.rem(t, z.n_head))

    def in_sequence(self, t):
        return (self.d, t // self.z.n_head, lax.rem(t, self.z.n_head))

    def owns(self, n):
        return self.active & (self.hd == n)

    def group(self, k):
        z = self.z
        e = lax.rem(self.g + k, z.NG)
        return e, (e // z.n_blk, lax.rem(e, z.n_blk), self.h)


def written(r, *names):
    for name in names:
        short = name.replace("_ref", "").replace("_out", "") + "_v"
        c = pltpu.make_async_copy(
            getattr(r, short), getattr(r, name), r.out_sem.at[PASSED.index(name)]
        )
        c.start()
        r.outgoing.append(c)


def layer_kernel(z, names, *refs):
    r = types.SimpleNamespace(**dict(zip(names, refs)))
    r.dkv = r.s_scr.at[:, pl.ds(0, 2 * HEAD_SIZE)]
    r.outgoing = []
    p = Place(z)

    def greet(k, carry):
        signal(p.any_peer(k)[1])
        return carry

    lax.fori_loop(1, z.ndev, greet, 0)
    D = z.D
    small = [
        pltpu.make_async_copy(ref, r.w_own.at[:, pl.ds(m * D, D)], r.in_sem.at[m])
        for m, ref in enumerate((r.wq_ref, r.wk_ref, r.wv_ref, r.wo_ref))
    ]
    small.append(pltpu.make_async_copy(r.x_ref, r.x_own, r.in_sem.at[4]))
    later = [
        pltpu.make_async_copy(r.cot_ref, r.cot, r.in_sem.at[5]),
        pltpu.make_async_copy(r.ids_ref, r.ids, r.in_sem.at[6]),
        pltpu.make_async_copy(r.win_ref.at[0], r.win, r.in_sem.at[7]),
        pltpu.make_async_copy(r.wout_ref.at[0], r.wout, r.in_sem.at[8]),
    ]
    for c in small + later:
        c.start()
    steps, finish_forward = forward_phase(z, r, p, small)
    for c in later:
        c.wait()
    last_slots, finish_middle = middle_phase(z, r, p, steps)
    backward_phase(z, r, p, steps, last_slots)
    finish_forward()
    finish_middle()
    for c in r.outgoing:
        c.wait()


def forward_phase(z, r, p, small):
    d, b, h, s, me, hd, active = p.d, p.b, p.h, p.s, p.me, p.hd, p.active
    hy, hc, hyc = p.hy, p.hc, p.hyc
    nb, nh, nd, ns = z.n_blk, z.n_head, z.n_dp, z.ns
    D, R, E, PT, HS = z.D, z.R, z.E, z.PT, HEAD_SIZE

    await_barrier(z.ndev - 1)
    small[4].wait()

    tokens = Sends(r.x_s)
    pieces = 2
    rows_of = PT // pieces

    def xref(slot, c):
        return r.xg.at[slot, pl.ds(c * rows_of, rows_of)]

    def put(src, slot, c, device, cond=None):
        tokens.put(src, xref(slot, c), r.x_r.at[slot * pieces + c], device, cond)

    def got(slot, c):
        ref = xref(slot, c)
        remote(ref, ref, r.x_s.at[0], r.x_r.at[slot * pieces + c], (d, b, hc)).wait_recv()

    for c in range(pieces):
        own = r.x_own.at[pl.ds(c * rows_of, rows_of)]
        put(own, s, c, (d, b + 1, h), b + 1 < nb)
        put(own, s, c, (d, b - 1, h), b >= 1)
        put(own, s, c, (d, b, hy))
        put(own, s, c, (d, b, hc))
    r.xg[s] = r.x_own[...]

    for c in small[:4]:
        c.wait()
    eye = lax.broadcasted_iota(jnp.int32, (R, R), 0) == lax.broadcasted_iota(jnp.int32, (R, R), 1)
    row_of = lax.broadcasted_iota(jnp.int32, (LANES, R), 0)
    tail = jnp.zeros((LANES, R), F32)
    rel = jnp.concatenate([r.rel_ref[...].astype(F32), jnp.zeros((1, R - z.RL), F32)], axis=1)
    rows = r.gain1_in[...].astype(F32), r.gain2_in[...].astype(F32), rel
    for n in range(3):
        tail = jnp.where(row_of == E + n, rows[n], tail)
    router_t = jnp.concatenate(
        [r.router_ref[...].astype(F32), jnp.zeros((LANES - E, R), F32)], axis=0
    )
    misc = nt(eye.astype(BF16), (tail + router_t).astype(BF16)).astype(BF16)
    r.w_own[:, 4 * D :] = misc
    for n in range(HEAD_COUNT):
        columns = [r.w_own[:, m * D + n * HS : m * D + (n + 1) * HS] for m in range(3)]
        r.slices[n] = jnp.concatenate(columns + [misc[:, E : E + HS]], axis=1)
    save_w = pltpu.make_async_copy(r.w_own, r.wg_ref.at[me], r.loc.at[0])
    save_w.start()
    to_heads = Sends(r.sl_s)
    over_dp = Sends(r.sd_s)
    for n in range(HEAD_COUNT):
        hb, hh = z.holder(n)
        to_heads.put(
            r.slices.at[n], r.slices_in.at[me], r.sl_r.at[me], (d, hb, hh),
            jnp.logical_not(p.owns(n)),
        )

    @pl.when(active)
    def _():
        r.slices_in[me] = r.slices[hd]

    for k in range(1, nb):
        for c in range(pieces):
            for f, cond, to, more in (
                (b - k, b >= k, b + 1, b + 1 < nb),
                (b + k, b + k < nb, b - 1, b >= 1),
            ):
                slot = f * nh + h
                pl.when(cond)(functools.partial(got, slot, c))
                if k < nb - 1:
                    put(xref(slot, c), slot, c, (d, to, h), cond & more)
                put(xref(slot, c), slot, c, (d, b, hy), cond)
                put(xref(slot, c), slot, c, (d, b, hc), cond)
        if k == 1:
            for m in range(ns):
                t = lax.rem(s + m, ns)
                slot = d * ns + t
                ref = r.slices_in.at[slot]
                if m > 0:
                    c = remote(ref, ref, r.sl_s.at[0], r.sl_r.at[slot], p.in_sequence(t))
                    pl.when(active)(c.wait_recv)
                for kd in range(1, nd):
                    over_dp.put(ref, ref, r.sl_r.at[slot], (lax.rem(d + kd, nd), b, h), active)

    for f, cond in line_order(b, nb):
        for c in range(pieces):
            slot = f * nh + hy
            pl.when(cond)(functools.partial(got, slot, c))
            put(xref(slot, c), slot, c, (d, b, hc), cond)

    cuts = (3 * D, z.wide, False), (0, 3 * D // 2, True), (3 * D // 2, 3 * D, False)
    parts = [
        Spread(
            z, r.w_own.at[:, pl.ds(lo, hi - lo)], r.wg_ref,
            getattr(r, "w%d_s" % n), getattr(r, "w%d_r" % n), y_first, pl.ds(lo, hi - lo),
        )
        for n, (lo, hi, y_first) in enumerate(cuts)
    ]
    first, rest_a, rest_b = [part.steps() for part in parts]
    steps = []
    for k in range(nb):
        steps += [first.pop(0), rest_a.pop(0), rest_b.pop(0)]
    steps = Steps(steps + first, rest_a, rest_b, parts, save_w)

    steps.run(3)

    @pl.when(active)
    def _():
        for kd in range(1, nd):
            dd = lax.rem(d + kd, nd)

            def got_slice(t, carry):
                ref = r.slices_in.at[dd * ns + t]
                remote(ref, ref, r.sl_s.at[0], r.sl_r.at[dd * ns + t], (dd, b, h)).wait_recv()
                return carry

            lax.fori_loop(0, ns, got_slice, 0)

        rows = flatten_rows(r.slices_in[...])
        r.wh[:, : 2 * HS] = rows[:, : 2 * HS].astype(BF16)
        r.wh[:, :HS] = (rows[:, :HS] * HS ** (-0.5)).astype(BF16)
        r.wh[:, 2 * HS :] = rows[:, 2 * HS : 3 * HS].astype(BF16)
        r.gain1[...] = jnp.transpose(rows[:, LANES:])[HS : HS + 1, :]
        column = lax.broadcasted_iota(jnp.int32, (1, D), 1).astype(F32)
        owner = jnp.floor((column + 0.5) * (1.0 / R))
        place_of = column - owner * R
        entry = jnp.where(place_of < z.RL, owner * z.RL + place_of, -1.0)
        wanted = hd * BUCKETS + lax.broadcasted_iota(jnp.int32, (BUCKETS, D), 0)
        pick = (entry == wanted.astype(F32)).astype(BF16)
        table = nn(pick, rows[:, LANES:].astype(BF16))[:, HS + 2 : HS + 3]
        r.bias_d[...] = bias_tile(table, 0)
        r.bias_s[...] = bias_tile(table, -BLOCK)
        r.far_bias[...] = table[BUCKETS // 2 - 1 : BUCKETS // 2, 0:1]

    for f in range(nb):
        for c in range(pieces):
            got(f * nh + hc, c)
            got(f * nh + hyc, c)
    tokens.finish()
    per = z.per
    half = BLOCK // 2

    @pl.when(active)
    def _():
        def project(i, carry):
            here = pl.ds(pl.multiple_of(i * BLOCK, BLOCK), BLOCK)
            own = pl.ds(i * per, per)
            x = r.xg[own].reshape(BLOCK, D).astype(F32)
            inverse = lax.rsqrt(jnp.mean(x * x, axis=-1, keepdims=True) + EPSILON)
            low = (x * inverse * r.gain1[...]).astype(BF16)
            r.xg[own] = low.reshape(per, PT, D)
            mixed = nn(low, r.wh[...])
            r.qkv[here, :] = mixed.astype(BF16)
            r.v_t[:, here] = jnp.transpose(mixed[:, 2 * HS :]).astype(BF16)
            r.k_t[:, here] = jnp.transpose(mixed[:, HS : 2 * HS]).astype(BF16)
            return carry

        lax.fori_loop(0, z.nq, project, 0)

    def send_att(t):
        return remote(
            r.att_src.at[t], r.att_in.at[hd], r.at_s.at[t], r.at_r.at[hd], (d, t // nh, t % nh)
        )

    low_rows, high_rows = range(z.nq // 2), range(z.nq // 2, z.nq)
    order = [i for pair in zip(reversed(high_rows), reversed(low_rows)) for i in pair]
    for i in order:
        steps.run(4)

        @pl.when(active)
        def _():
            here = slice(i * BLOCK, (i + 1) * BLOCK)
            q = r.qkv[here, :HS]
            top = jnp.full((8, BLOCK), -1e30, F32)
            far = r.far_bias[...]
            for j in range(i + 1):
                for u in range(2):
                    at = slice(j * BLOCK + u * half, j * BLOCK + (u + 1) * half)
                    part = slice(u * half, (u + 1) * half)
                    if j == i:
                        bias = r.bias_d[part, :]
                    elif j == i - 1:
                        bias = r.bias_s[part, :]
                    else:
                        bias = far
                    sc = nt(r.qkv[at, HS : 2 * HS], q) + bias
                    r.s_scr[at, :] = sc
                    top = jnp.maximum(top, jnp.max(sc.reshape(half // 8, 8, BLOCK), axis=0))
            top = jnp.max(top, axis=0, keepdims=True)
            total = jnp.zeros((8, BLOCK), F32)
            acc = jnp.zeros((HS, BLOCK), F32)
            for j in range(i + 1):
                for u in range(2):
                    at = slice(j * BLOCK + u * half, j * BLOCK + (u + 1) * half)
                    e = jnp.exp(r.s_scr[at, :] - top)
                    total = total + jnp.sum(e.reshape(half // 8, 8, BLOCK), axis=0)
                    r.probs[i, at, :] = e.astype(BF16)
                at = slice(j * BLOCK, (j + 1) * BLOCK)
                acc = acc + nn(r.v_t[:, at], r.probs[i, at, :])
            total = jnp.sum(total, axis=0, keepdims=True)
            both = jnp.concatenate([acc, jnp.broadcast_to(total, (HS, BLOCK))], axis=0)
            both = jnp.transpose(both)
            inv = 1.0 / both[:, HS:]
            att = (both[:, :HS] * inv).astype(BF16)
            r.attl[here, :] = jnp.concatenate([att.astype(F32), inv], axis=1)
            for u in range(per):
                t = i * per + u
                r.att_src[t] = both_halves(att[u * PT : (u + 1) * PT])

                @pl.when(t != s)
                def _():
                    send_att(t).start()

                @pl.when(t == s)
                def _():
                    r.att_in[hd] = r.att_src[t]

    def finish():
        to_heads.finish()
        over_dp.finish()

        @pl.when(active)
        def _():
            for t in range(ns):

                @pl.when(t != s)
                def _():
                    send_att(t).wait_send()

    return steps, finish


class Steps:
    def __init__(self, first, rest_a, rest_b, parts, save):
        self.first, self.parts, self.save = first, parts, save
        self.rest = [
            step
            for pair in itertools.zip_longest(rest_b, rest_a)
            for step in pair
            if step is not None
        ]

    def run(self, count):
        for _ in range(min(count, len(self.first))):
            self.first.pop(0)()

    def finish_first(self):
        self.run(len(self.first))
        self.parts[0].finish()
        self.save.wait()

    def run_rest(self, count):
        for _ in range(min(count, len(self.rest))):
            self.rest.pop(0)()

    def finish_rest(self):
        self.run_rest(len(self.rest))
        for part in self.parts[1:]:
            part.finish()


def middle_phase(z, r, p, steps):
    d, b, h, me, g, s = p.d, p.b, p.h, p.me, p.g, p.s
    hy, hc, hyc = p.hy, p.hc, p.hyc
    nb, nh, nd, ns = z.n_blk, z.n_head, z.n_dp, z.ns
    D, E, PT, NG, C8 = z.D, z.E, z.PT, z.NG, z.cap8

    ids_row = r.ids[pl.ds(me, 1), :]
    order_row = r.order_ref[...]
    ids_col = jnp.transpose(jnp.broadcast_to(ids_row, (PT, PT)))
    order_col = jnp.transpose(jnp.broadcast_to(order_row, (PT, PT)))
    earlier = (order_col < order_row) & (ids_col == ids_row)
    rank = jnp.sum(earlier.astype(jnp.int32), axis=0, keepdims=True)
    slot = lax.broadcasted_iota(jnp.int32, (C8, PT), 0)
    base = (rank == slot) & (slot < z.cap)
    lane = lax.broadcasted_iota(jnp.int32, (1, LANES), 1)
    share = jnp.zeros((1, LANES), F32)
    ids_all = r.ids[...]
    for e in range(E):
        r.route[e * C8 : (e + 1) * C8, :] = (base & (ids_row == e)).astype(F32)
        count = jnp.sum((ids_all == e).astype(F32), axis=1, keepdims=True)
        count = jnp.sum(count, axis=0, keepdims=True)
        share = share + jnp.where(lane == e, count, 0.0)
    share = share * (AUX_WEIGHT * E / (ids_all.shape[0] * ids_all.shape[1]))
    chosen = ids_col[:, :1] == lane
    picks = r.route[...].astype(BF16)
    x = r.x_own[...].astype(F32)
    cot = r.cot[...].astype(F32)

    steps.finish_first()
    load = [
        pltpu.make_async_copy(r.wg_ref.at[:, :, pl.ds(3 * D, D)], r.w3.at[0], r.loc.at[1]),
        pltpu.make_async_copy(r.wg_ref.at[:, :, pl.ds(4 * D, LANES)], r.misc3, r.loc.at[2]),
    ]
    for c in load:
        c.start()
    for c in load:
        c.wait()
    r.wo[...] = flatten_rows(r.w3[0]).astype(BF16)
    misc = flatten_rows(r.misc3[...])
    router = misc.astype(BF16)
    lines = jnp.transpose(misc)
    r.gain1[...] = lines[E : E + 1, :]
    gain = lines[E + 1 : E + 2, :]
    for n in range(HEAD_COUNT):
        hb, hh = z.holder(n)

        @pl.when(jnp.logical_not(p.owns(n)))
        def _():
            ref = r.att_in.at[n]
            remote(ref, ref, r.at_s.at[0], r.at_r.at[n], (d, hb, hh)).wait_recv()

        at = slice(n * HEAD_SIZE, (n + 1) * HEAD_SIZE)
        r.att_cat[: PT // 2, at] = r.att_in[n, :, :HEAD_SIZE]
        r.att_cat[PT // 2 :, at] = r.att_in[n, :, HEAD_SIZE:]
    att = r.att_cat[...]
    middle = x + nn(att, r.wo[...])
    inverse = lax.rsqrt(jnp.mean(middle * middle, axis=-1, keepdims=True) + EPSILON)
    routed = (middle * inverse * gain).astype(BF16)

    out = Sends(r.ex_s)

    def dispatch(part, values):
        r.disp[part] = nn(picks, values).reshape(E, C8, D).astype(BF16)
        for k in range(1, NG):
            e, device = p.group(k)
            out.put(r.disp.at[part, e], r.exp_in.at[part, g], r.ex_r.at[part * NG + g], device)
        r.exp_in[part, g] = r.disp[part, g]

    def arrivals(part):
        for k in range(1, NG):
            e, device = p.group(NG - k)
            ref = r.exp_in.at[part, e]
            remote(ref, ref, r.ex_s.at[0], r.ex_r.at[part * NG + e], device).wait_recv()

    def give_back(part, values):
        r.ret[part] = values.reshape(NG, C8, D).astype(BF16)
        for k in range(1, NG):
            e, device = p.group(k)
            out.put(r.ret.at[part, e], r.back.at[part, g], r.rt_r.at[part * NG + g], device)
        r.back[part, g] = r.ret[part, g]

    def returns(part):
        for k in range(1, NG):
            e, device = p.group(NG - k)
            ref = r.back.at[part, e]
            remote(ref, ref, r.ex_s.at[0], r.rt_r.at[part * NG + e], device).wait_recv()
        rows = r.back[part].astype(F32).reshape(E * C8, D).astype(BF16)
        return tn(picks, rows)

    copies = []

    def share_slots(part):
        src, dst, sem = r.exp_in.at[part], r.slots_ref.at[part, h], r.all_r.at[part * nh + h]
        out.put(src, dst, sem, (d, b, hy))
        out.put(src, dst, sem, (d, b, hc))
        c = pltpu.make_async_copy(src, dst, r.loc.at[3 + part])
        c.start()
        copies.append(c)

    def got_slots(part, hh):
        ref = r.slots_ref.at[part, hh]
        remote(ref, ref, r.ex_s.at[0], r.all_r.at[part * nh + hh], (d, b, hc)).wait_recv()

    dispatch(0, routed)
    logits = jnp.where(lane < E, nn(routed, router), -1e30)
    exps = jnp.exp(logits - jnp.max(logits, axis=-1, keepdims=True))
    probs = exps / jnp.sum(exps, axis=-1, keepdims=True)
    gate = jnp.sum(jnp.where(chosen, probs, 0.0), axis=-1, keepdims=True)
    dispatch(1, (gate * cot).astype(BF16))
    chunk = D // 2
    chunks = z.FF // chunk
    steps.run_rest(14)

    arrivals(0)
    share_slots(0)
    rows_in = r.exp_in[0].astype(F32).reshape(NG * C8, D).astype(BF16)
    r.out_acc[...] = jnp.zeros_like(r.out_acc)

    def forward_step(c, carry):
        at = pl.ds(pl.multiple_of(c * chunk, chunk), chunk)
        pre = nn(rows_in, r.win[:, at])
        hidden, r.slope[:, at] = activate(pre)
        r.hid[:, at] = hidden
        r.out_acc[...] += nn(hidden, r.wout[at, :])
        return carry

    lax.fori_loop(0, chunks, forward_step, 0)
    give_back(0, r.out_acc[...])

    arrivals(1)
    share_slots(1)
    grad_out = r.exp_in[1].astype(F32).reshape(NG * C8, D).astype(BF16)
    r.out_acc[...] = jnp.zeros_like(r.out_acc)

    def backward_step(c, carry):
        at = pl.ds(pl.multiple_of(c * chunk, chunk), chunk)
        gp = grad_pre(grad_out, r.wout[at, :], r.slope[:, at])
        r.slope[:, at] = gp
        r.out_acc[...] += nt(gp, r.win[:, at])
        return carry

    lax.fori_loop(0, chunks, backward_step, 0)
    give_back(1, r.out_acc[...])
    saves = []

    def save(hh):
        for n, (src, dst) in enumerate(((r.hid, r.hid_ref), (r.slope, r.gp_ref))):
            c = pltpu.make_async_copy(src, dst.at[hh], r.loc.at[8 + n])
            c.start()
            saves.append(c)

    def other_slots(hh, forward):
        for part in range(2):
            got_slots(part, hh)
            if forward:
                ref = r.slots_ref.at[part, hh]
                out.put(ref, ref, r.all_r.at[part * nh + hh], (d, b, hc))
        c = pltpu.make_async_copy(r.slots_ref.at[:, hh], r.act_in, r.loc.at[10])
        c.start()
        c.wait()
        while saves:
            saves.pop().wait()
        others_in = r.act_in[0].astype(F32).reshape(NG * C8, D).astype(BF16)
        others_grad = r.act_in[1].astype(F32).reshape(NG * C8, D).astype(BF16)

        def step(c, carry):
            at = pl.ds(pl.multiple_of(c * chunk, chunk), chunk)
            r.hid[:, at], slope = activate(nn(others_in, r.win[:, at]))
            r.slope[:, at] = grad_pre(others_grad, r.wout[at, :], slope)
            return carry

        lax.fori_loop(0, chunks, step, 0)
        save(hh)

    save(h)
    steps.run_rest(10)
    for c in copies:
        c.wait()
    other_slots(hc, False)

    expert_rows = returns(0)
    r.layer_v[...] = (middle + gate * expert_rows).astype(BF16)
    written(r, "layer_ref")
    grad_gate = jnp.sum(cot * expert_rows, axis=-1, keepdims=True)
    grad_probs = jnp.where(chosen, grad_gate, 0.0) + share
    inner = jnp.sum(probs * grad_probs, axis=-1, keepdims=True)
    grad_logits = (probs * (grad_probs - inner)).astype(BF16)
    from_router = nt(grad_logits, router)
    grad_routed = returns(1) + from_router
    scaled = grad_routed * gain
    mean = jnp.mean(scaled * middle, axis=-1, keepdims=True)
    gmid = cot + inverse * scaled - middle * (inverse * inverse * inverse) * mean
    r.gmid[...] = gmid
    low_mid = gmid.astype(BF16)
    gatt = nt(low_mid, r.wo[...]).astype(BF16)

    for n in range(HEAD_COUNT):
        r.gatt[n] = both_halves(gatt[:, n * HEAD_SIZE : (n + 1) * HEAD_SIZE])
        hb, hh = z.holder(n)
        out.put(
            r.gatt.at[n], r.do_in.at[s], r.do_r.at[s], (d, hb, hh), jnp.logical_not(p.owns(n))
        )

        @pl.when(p.owns(n))
        def _():
            r.do_in[s] = r.gatt[n]

    term = grad_routed * middle * inverse
    high = term.astype(BF16)
    rest = (term - high.astype(F32)).astype(BF16)
    ones = jnp.broadcast_to((lane == E).astype(BF16), (PT, LANES))
    small = tn(routed, grad_logits) + tn(high, ones) + tn(rest, ones)
    terms = jnp.concatenate([tn(att, low_mid), small], axis=1)
    for t in range(z.ndev):
        r.dwo[t % nh, t // nh] = terms[t * z.R : (t + 1) * z.R].astype(BF16)
    other_slots(hy, True)

    def finish():
        while saves:
            saves.pop().wait()
        out.finish()

    return functools.partial(other_slots, hyc, False), finish


def backward_phase(z, r, p, steps, last_slots):
    d, b, h, s, me, hd, active = p.d, p.b, p.h, p.s, p.me, p.hd, p.active
    hy, hc, hyc = p.hy, p.hc, p.hyc
    nb, nh, nd, ns, nv, NG = z.n_blk, z.n_head, z.n_dp, z.ns, z.ndev, z.NG
    D, R, PT, HS, E = z.D, z.R, z.PT, HEAD_SIZE, z.E

    def sum_in(dst, src, terms, count):
        def body(e, carry):
            acc = src(e).astype(F32)
            for term in terms:
                acc = acc + term(e).astype(F32)
            dst[e] = acc.astype(BF16)
            return carry

        lax.fori_loop(0, count, body, 0)

    sums = Sends(r.su_s)
    y_sum = r.core_in.at[0]

    def got_sum(ref, k):
        remote(ref, ref, r.su_s.at[0], r.su_r.at[k], (d, b, hc)).wait_recv()

    def stage_core():
        sums.put(r.dwo.at[hyc], r.core_in.at[0], r.su_r.at[0], (d, b, hc))
        sums.put(r.dwo.at[hc], r.core_in.at[1], r.su_r.at[1], (d, b, hc))

    def stage_y():
        got_sum(r.core_in.at[0], 0)
        sum_in(r.y_src, lambda e: r.dwo[hy, e], [lambda e: r.core_in[0, e]], NG)
        sums.put(r.y_src, r.y_in, r.su_r.at[2], (d, b, hy))

    def stage_dp():
        got_sum(r.core_in.at[1], 1)
        got_sum(r.y_in, 2)
        sum_in(
            y_sum, lambda e: r.dwo[h, e], [lambda e: r.core_in[1, e], lambda e: r.y_in[e]], NG
        )
        for k in range(1, nd):
            q = lax.rem(d + k, nd)
            sums.put(y_sum.at[pl.ds(q * nb, nb)], r.dp_in.at[d], r.su_r.at[3 + d], (q, b, h))

    def stage_blk():
        others = [lax.rem(d + k, nd) for k in range(1, nd)]
        for q in others:
            got_sum(r.dp_in.at[q], 3 + q)

        def body(e, carry):
            acc = y_sum[d * nb + e].astype(F32)
            for q in others:
                acc = acc + r.dp_in[q, e].astype(F32)
            r.blk_src[e] = acc.astype(BF16)
            return carry

        lax.fori_loop(0, nb, body, 0)
        for k in range(1, nb):
            e = lax.rem(b + k, nb)
            sums.put(r.blk_src.at[e], r.blk_in.at[b], r.su_r.at[3 + nd + b], (d, e, h))
        r.blk_in[b] = r.blk_src[b]

    stage_core()

    def send_dq(t):
        return remote(
            r.dqkv.at[t], r.dq_in.at[hd], r.dq_s.at[t], r.dq_r.at[hd], (d, t // nh, t % nh)
        )

    def send_dw(k):
        t, device = p.any_peer(k)
        slot = d * HEAD_COUNT + hd
        return remote(r.dw3.at[t], r.dw_in.at[slot], r.dw_s.at[k], r.dw_r.at[slot], device)

    per = z.per
    part_rows = BLOCK // 2

    @pl.when(active)
    def _():
        r.dkv[...] = jnp.zeros_like(r.dkv)
        r.dq_acc[...] = jnp.zeros_like(r.dq_acc)
        r.dw[...] = jnp.zeros_like(r.dw)
        r.diag[...] = jnp.zeros_like(r.diag)
        r.sub[...] = jnp.zeros_like(r.sub)
        r.far[...] = jnp.zeros_like(r.far)

        def got_do(k, carry):
            t = lax.rem(s + k, ns)
            ref = r.do_in.at[t]
            remote(ref, ref, r.ex_s.at[0], r.do_r.at[t], p.in_sequence(t)).wait_recv()
            return carry

        lax.fori_loop(1, ns, got_do, 0)
        ones = jnp.ones((8, HS), BF16)

        def prepare(i, carry):
            here = pl.ds(pl.multiple_of(i * BLOCK, BLOCK), BLOCK)
            pairs = [r.do_in[i * per + u] for u in range(per)]
            do = jnp.concatenate(
                [side for pair in pairs for side in (pair[:, :HS], pair[:, HS:])], axis=0
            )
            do = (do.astype(F32) * r.attl[here, HS:]).astype(BF16)
            r.dos[here, :] = do
            prod = do.astype(F32) * r.attl[here, :HS]
            high = prod.astype(BF16)
            rest = (prod - high.astype(F32)).astype(BF16)
            r.delta[i] = nt(ones, high) + nt(ones, rest)
            return carry

        lax.fori_loop(0, z.nq, prepare, 0)

    def tile(i, j, u):
        at = slice(j * BLOCK + u * part_rows, j * BLOCK + (u + 1) * part_rows)
        here = slice(i * BLOCK, (i + 1) * BLOCK)
        pr = r.probs[i, at, :]
        do = r.dos[here, :]
        ds = pr.astype(F32) * (nt(r.qkv[at, 2 * HS :], do) - r.delta[i, 0:1, :])
        low = ds.astype(BF16)
        part = slice(u * part_rows, (u + 1) * part_rows)
        if j == i:
            r.diag[part, :] += low.astype(F32)
        elif j == i - 1:
            r.sub[part, :] += low.astype(F32)
        else:
            r.far[...] += jnp.sum(low.astype(F32).reshape(part_rows // 8, 8, BLOCK), axis=0)
        both = jnp.concatenate([nn(low, r.qkv[here, :HS]), nn(pr, do)], axis=1)
        return at, both, nn(r.k_t[:, at], low)

    def column(j, hi):
        for u in range(2):
            acc = jnp.zeros((part_rows, 2 * HS), F32)
            for i in range(j, hi + 1):
                at, both, dq = tile(i, j, u)
                acc = acc + both
                r.dq_acc[i] += dq
            r.dkv[at, :] += acc

    def row(i, lo):
        acc = jnp.zeros((HS, BLOCK), F32)
        for j in range(lo, i + 1):
            for u in range(2):
                at, both, dq = tile(i, j, u)
                r.dkv[at, :] += both
                acc = acc + dq
        r.dq_acc[i] += acc

    lo, hi = 0, z.nq - 1
    turn = 0
    while lo <= hi:
        if turn == 1:
            stage_y()
        if turn == 3:
            stage_dp()
        if turn == z.nq - 1:
            stage_blk()

        @pl.when(active)
        def _():
            if turn % 2 == 0:
                n = lo
                column(n, hi)
            else:
                n = hi
                row(n, lo)
            here = slice(n * BLOCK, (n + 1) * BLOCK)
            dq = jnp.transpose(r.dq_acc[n]) * HS ** (-0.5)
            parts = jnp.concatenate([dq, r.dkv[here, :]], axis=1).astype(BF16)
            r.dw[...] += tn(r.xg[n * per : (n + 1) * per].reshape(BLOCK, D), parts)
            for u in range(per):
                t = n * per + u
                piece = parts[u * PT : (u + 1) * PT]
                r.dqkv[t, :PT] = piece[:, : 2 * HS]
                r.dqkv[t, PT:] = both_halves(piece[:, 2 * HS :])

                @pl.when(t != s)
                def _():
                    send_dq(t).start()

                @pl.when(t == s)
                def _():
                    r.dq_in[hd] = r.dqkv[t]

        if turn % 2 == 0:
            lo += 1
        else:
            hi -= 1
        turn += 1
        steps.run_rest(6)

    @pl.when(active)
    def _():
        lane = lax.broadcasted_iota(jnp.int32, (1, HS), 1)
        half = BUCKETS // 2
        sums_of = bucket_sums(r.diag[...], 0) + bucket_sums(r.sub[...], BLOCK)
        beyond = jnp.sum(jnp.sum(r.far[...], axis=0, keepdims=True), axis=1, keepdims=True)
        sums_of = sums_of + jnp.where(lane == half - 1, beyond, 0.0)
        wide = jnp.concatenate([r.dw[...], jnp.broadcast_to(sums_of, (D, HS))], axis=1)
        split_rows(r.dw3, wide, R)

        def start_dw(k, carry):
            send_dw(k).start()
            return carry

        lax.fori_loop(1, nv, start_dw, 0)
        r.dw_in[d * HEAD_COUNT + hd] = r.dw3[me]

    last_slots()
    steps.finish_rest()
    load = [
        pltpu.make_async_copy(r.wg_ref.at[:, :, pl.ds(m * D, D)], r.w3.at[m], r.loc.at[5 + m])
        for m in range(3)
    ]
    for c in load:
        c.start()
    for m, c in enumerate(load):
        c.wait()
        r.wfull[:, m * D : (m + 1) * D] = flatten_rows(r.w3[m]).astype(BF16)

    for k in range(1, nb):
        e = lax.rem(b + k, nb)
        got_sum(r.blk_in.at[e], 3 + nd + e)
    acc = r.blk_in[0].astype(F32)
    for e in range(1, nb):
        acc = acc + r.blk_in[e].astype(F32)
    eye = lax.broadcasted_iota(jnp.int32, (R, R), 0) == lax.broadcasted_iota(jnp.int32, (R, R), 1)

    def as_row(column):
        return jnp.sum(jnp.where(eye, column, 0.0), axis=0, keepdims=True)

    r.go_v[...] = acc[:, :D]
    r.router_v[...] = jnp.concatenate([as_row(acc[:, D + e : D + e + 1]) for e in range(E)], axis=0)
    r.gain2_v[...] = as_row(acc[:, D + E : D + E + 1])
    written(r, "go_ref", "router_out", "gain2_ref")

    for n in range(HEAD_COUNT):
        hb, hh = z.holder(n)

        @pl.when(jnp.logical_not(p.owns(n)))
        def _():
            ref = r.dq_in.at[n]
            remote(ref, ref, r.dq_s.at[0], r.dq_r.at[n], (d, hb, hh)).wait_recv()

        for m in range(2):
            r.grad_cat[:, m * D + n * HS : m * D + (n + 1) * HS] = r.dq_in[
                n, :PT, m * HS : (m + 1) * HS
            ]
        at = slice(2 * D + n * HS, 2 * D + (n + 1) * HS)
        r.grad_cat[: PT // 2, at] = r.dq_in[n, PT:, :HS]
        r.grad_cat[PT // 2 :, at] = r.dq_in[n, PT:, HS:]
    grad_normed = nt(r.grad_cat[...], r.wfull[...])
    x = r.x_own[...].astype(F32)
    inverse = lax.rsqrt(jnp.mean(x * x, axis=-1, keepdims=True) + EPSILON)
    scaled = grad_normed * r.gain1[...]
    mean = jnp.mean(scaled * x, axis=-1, keepdims=True)
    grad_in = inverse * scaled - x * (inverse * inverse * inverse) * mean
    r.gtok_v[...] = (r.gmid[...] + grad_in).astype(BF16)
    written(r, "gtok_ref")

    for dd in range(nd):
        for n in range(HEAD_COUNT):
            hb, hh = z.holder(n)

            @pl.when(jnp.logical_not(p.owns(n) & (d == dd)))
            def _():
                ref = r.dw_in.at[dd * HEAD_COUNT + n]
                remote(
                    ref, ref, r.dw_s.at[0], r.dw_r.at[dd * HEAD_COUNT + n], (dd, hb, hh)
                ).wait_recv()

    first = jnp.zeros((R, HS), F32)
    lines = []
    for n in range(HEAD_COUNT):
        part = r.dw_in[n].astype(F32)
        for dd in range(1, nd):
            part = part + r.dw_in[dd * HEAD_COUNT + n].astype(F32)
        for m, out in enumerate((r.gq_v, r.gk_v, r.gv_v)):
            cols = part[:, m * HS : (m + 1) * HS]
            out[:, n * HS : (n + 1) * HS] = cols
            own = r.w_own[:, m * D + n * HS : m * D + (n + 1) * HS].astype(F32)
            first = first + cols * own
        lines.append(part[0:1, 3 * HS : 3 * HS + BUCKETS])
    first = jnp.sum(first, axis=-1, keepdims=True)
    table = jnp.concatenate(lines, axis=0)
    entry = lax.broadcasted_iota(jnp.int32, table.shape, 0) * BUCKETS + lax.broadcasted_iota(
        jnp.int32, table.shape, 1
    )
    slot_lane = lax.broadcasted_iota(jnp.int32, (1, z.RL), 1)
    own_table = jnp.zeros((1, z.RL), F32)
    for k in range(z.RL):
        value = jnp.sum(jnp.where(entry == me * z.RL + k, table, 0.0), axis=0, keepdims=True)
        value = jnp.sum(value, axis=1, keepdims=True)
        own_table = own_table + jnp.where(slot_lane == k, value, 0.0)
    own_gain = r.w_own[:, 4 * D :].astype(F32)[:, E : E + 1]
    r.gain1_v[...] = as_row(first / own_gain)
    r.table_v[...] = own_table
    written(r, "gain1_ref", "gq_ref", "gk_ref", "gv_ref", "table_ref")

    sums.finish()

    @pl.when(active)
    def _():
        for t in range(ns):

            @pl.when(t != s)
            def _():
                send_dq(t).wait_send()

        def sent_dw(k, carry):
            send_dw(k).wait_send()
            return carry

        lax.fori_loop(1, nv, sent_dw, 0)


def layer(z, x, order, ids, rows, weights, router_t, w_in, w_out, cot):
    D, R, PT, S, HS, E, NG, C8 = z.D, z.R, z.PT, z.S, HEAD_SIZE, z.E, z.NG, z.cap8
    nb, nd, nh, ns, nv = z.n_blk, z.n_dp, z.n_head, z.ns, z.ndev
    dma = pltpu.SemaphoreType.DMA
    vmem = pl.BlockSpec(memory_space=pltpu.VMEM)
    hbm = pl.BlockSpec(memory_space=pltpu.HBM)
    shape = jax.ShapeDtypeStruct
    inputs = {
        "x_ref": (x, hbm),
        "order_ref": (order, vmem),
        "ids_ref": (ids, hbm),
        "gain1_in": (rows[0][None, :], vmem),
        "gain2_in": (rows[1][None, :], vmem),
        "rel_ref": (rows[2][None, :], vmem),
        "wq_ref": (weights[0], hbm),
        "wk_ref": (weights[1], hbm),
        "wv_ref": (weights[2], hbm),
        "wo_ref": (weights[3], hbm),
        "router_ref": (router_t, vmem),
        "win_ref": (w_in, hbm),
        "wout_ref": (w_out, hbm),
        "cot_ref": (cot, hbm),
    }
    outputs = {
        "wg_ref": (shape((nv, R, z.wide), BF16), hbm),
        "slots_ref": (shape((2, nh, NG, C8, D), BF16), hbm),
        "hid_ref": (shape((nh, NG * C8, z.FF), BF16), hbm),
        "gp_ref": (shape((nh, NG * C8, z.FF), BF16), hbm),
        "layer_ref": (shape((PT, D), BF16), hbm),
        "gtok_ref": (shape((PT, D), BF16), hbm),
        "gain1_ref": (shape((1, R), F32), hbm),
        "gq_ref": (shape((R, D), F32), hbm),
        "gk_ref": (shape((R, D), F32), hbm),
        "gv_ref": (shape((R, D), F32), hbm),
        "go_ref": (shape((R, D), F32), hbm),
        "table_ref": (shape((1, z.RL), F32), hbm),
        "gain2_ref": (shape((1, R), F32), hbm),
        "router_out": (shape((E, R), F32), hbm),
    }
    V = pltpu.VMEM
    terms = D + LANES
    scratch = {
        "w_own": V((R, z.wide), BF16),
        "x_own": V((PT, D), BF16),
        "cot": V((PT, D), BF16),
        "ids": V(ids.shape, jnp.int32),
        "win": V((D, z.FF), BF16),
        "wout": V((z.FF, D), BF16),
        "slices": V((HEAD_COUNT, R, 4 * HS), BF16),
        "slices_in": V((nv, R, 4 * HS), BF16),
        "xg": V((ns, PT, D), BF16),
        "wh": V((D, 3 * HS), BF16),
        "gain1": V((1, D), F32),
        "far_bias": V((1, 1), F32),
        "bias_d": V((BLOCK, BLOCK), F32),
        "bias_s": V((BLOCK, BLOCK), F32),
        "qkv": V((S, 3 * HS), BF16),
        "v_t": V((HS, S), BF16),
        "k_t": V((HS, S), BF16),
        "s_scr": V((S, BLOCK), F32),
        "probs": V((z.nq, S, BLOCK), BF16),
        "attl": V((S, 2 * HS), F32),
        "att_src": V((ns, PT // 2, 2 * HS), BF16),
        "att_in": V((HEAD_COUNT, PT // 2, 2 * HS), BF16),
        "misc3": V((nv, R, LANES), BF16),
        "wo": V((D, D), BF16),
        "route": V((E * C8, PT), F32),
        "att_cat": V((PT, D), BF16),
        "disp": V((2, E, C8, D), BF16),
        "exp_in": V((2, NG, C8, D), BF16),
        "ret": V((2, NG, C8, D), BF16),
        "back": V((2, E, C8, D), BF16),
        "hid": V((NG * C8, z.FF), BF16),
        "slope": V((NG * C8, z.FF), BF16),
        "act_in": V((2, NG, C8, D), BF16),
        "out_acc": V((NG * C8, D), F32),
        "gmid": V((PT, D), F32),
        "gatt": V((HEAD_COUNT, PT // 2, 2 * HS), BF16),
        "do_in": V((ns, PT // 2, 2 * HS), BF16),
        "dwo": V((nh, NG, R, terms), BF16),
        "core_in": V((2, NG, R, terms), BF16),
        "y_src": V((NG, R, terms), BF16),
        "y_in": V((NG, R, terms), BF16),
        "dp_in": V((nd, nb, R, terms), BF16),
        "blk_src": V((nb, R, terms), BF16),
        "blk_in": V((nb, R, terms), BF16),
        "dos": V((S, HS), BF16),
        "delta": V((z.nq, 8, BLOCK), F32),
        "dq_acc": V((z.nq, HS, BLOCK), F32),
        "dw": V((D, 3 * HS), F32),
        "dw3": V((nv, R, 4 * HS), BF16),
        "diag": V((BLOCK, BLOCK), F32),
        "sub": V((BLOCK, BLOCK), F32),
        "far": V((8, BLOCK), F32),
        "dqkv": V((ns, PT + PT // 2, 2 * HS), BF16),
        "dq_in": V((HEAD_COUNT, PT + PT // 2, 2 * HS), BF16),
        "dw_in": V((nd * HEAD_COUNT, R, 4 * HS), BF16),
        "w3": V((3, nv, R, D), BF16),
        "wfull": V((D, 3 * D), BF16),
        "grad_cat": V((PT, 3 * D), BF16),
        "layer_v": V((PT, D), BF16),
        "gtok_v": V((PT, D), BF16),
        "gain1_v": V((1, R), F32),
        "gq_v": V((R, D), F32),
        "gk_v": V((R, D), F32),
        "gv_v": V((R, D), F32),
        "go_v": V((R, D), F32),
        "table_v": V((1, z.RL), F32),
        "gain2_v": V((1, R), F32),
        "router_v": V((E, R), F32),
        "out_sem": dma((len(PASSED),)),
        "in_sem": dma((9,)),
        "loc": dma((11,)),
        "sl_s": dma((HEAD_COUNT,)),
        "sl_r": dma((nv,)),
        "sd_s": dma((ns * nd,)),
        "x_s": dma((2 * (4 + 6 * (nb - 1) + 2 * nb - 1),)),
        "x_r": dma((2 * ns,)),
        "w0_s": dma((spread_copies(z, False),)),
        "w0_r": dma((nv,)),
        "w1_s": dma((spread_copies(z, True),)),
        "w1_r": dma((nv,)),
        "w2_s": dma((spread_copies(z, False),)),
        "w2_r": dma((nv,)),
        "at_s": dma((ns,)),
        "at_r": dma((HEAD_COUNT,)),
        "ex_s": dma((4 * (NG - 1) + 6 + HEAD_COUNT,)),
        "ex_r": dma((2 * NG,)),
        "rt_r": dma((2 * NG,)),
        "all_r": dma((2 * nh,)),
        "do_r": dma((ns,)),
        "su_s": dma((3 + nd - 1 + nb - 1,)),
        "su_r": dma((3 + nd + nb,)),
        "dq_s": dma((ns,)),
        "dq_r": dma((HEAD_COUNT,)),
        "dw_s": dma((nv,)),
        "dw_r": dma((nd * HEAD_COUNT,)),
    }
    names = tuple(inputs) + tuple(outputs) + tuple(scratch)
    results = pl.pallas_call(
        functools.partial(layer_kernel, z, names),
        out_shape=tuple(v[0] for v in outputs.values()),
        in_specs=[v[1] for v in inputs.values()],
        out_specs=tuple(v[1] for v in outputs.values()),
        scratch_shapes=list(scratch.values()),
        compiler_params=pltpu.CompilerParams(
            collective_id=0, has_side_effects=True, vmem_limit_bytes=VMEM_LIMIT
        ),
        name="layer",
    )(*[v[0] for v in inputs.values()])
    return dict(zip(outputs, results))


def expert_kernel(z, slots_ref, hid_ref, gp_ref, *refs):
    count = len(PASSED)
    passed_in, (gin_ref, gout_ref) = refs[:count], refs[count : count + 2]
    passed_out = refs[count + 2 : 2 * count + 2]
    rows_t, grad_out = refs[2 * count + 2 :]
    step = pl.program_id(0)

    @pl.when(step == 0)
    def _():
        for src, dst in zip(passed_in, passed_out):
            dst[...] = src[...]
        count = z.NG * z.cap8
        for n in range(z.n_head):
            at = slice(n * count, (n + 1) * count)
            rows_in = slots_ref[0, n].astype(F32).reshape(count, z.D)
            rows_t[:, at] = jnp.transpose(rows_in).astype(BF16)
            grad_out[at, :] = slots_ref[1, n].astype(F32).reshape(count, z.D).astype(BF16)

    total = z.n_head * z.NG * z.cap8
    chunk = hid_ref.shape[2]
    gin_ref[0] = nn(rows_t[...], gp_ref[...].reshape(total, chunk))
    gout_ref[0] = tn(hid_ref[...].reshape(total, chunk), grad_out[...])


def expert_weights(z, slots, hid, gp, passed):
    chunk = 768
    vmem = pl.BlockSpec(memory_space=pltpu.VMEM)
    total = z.n_head * z.NG * z.cap8
    in_chunk = pl.BlockSpec((1, z.D, chunk), lambda i: (0, 0, i))
    act_chunk = pl.BlockSpec((z.n_head, z.NG * z.cap8, chunk), lambda i: (0, 0, i))
    out_chunk = pl.BlockSpec((1, chunk, z.D), lambda i: (0, i, 0))
    return pl.pallas_call(
        functools.partial(expert_kernel, z),
        grid=(z.FF // chunk,),
        out_shape=(
            jax.ShapeDtypeStruct((1, z.D, z.FF), F32),
            jax.ShapeDtypeStruct((1, z.FF, z.D), F32),
        )
        + tuple(jax.ShapeDtypeStruct(a.shape, a.dtype) for a in passed),
        in_specs=[pl.BlockSpec(memory_space=pltpu.VMEM), act_chunk, act_chunk] + [vmem] * len(passed),
        out_specs=(in_chunk, out_chunk) + (vmem,) * len(passed),
        scratch_shapes=[
            pltpu.VMEM((z.D, total), BF16),
            pltpu.VMEM((total, z.D), BF16),
        ],
        compiler_params=pltpu.CompilerParams(
            dimension_semantics=("arbitrary",), vmem_limit_bytes=VMEM_LIMIT
        ),
        name="expert_weight_grads",
    )(slots, hid, gp, *passed)


def local(
    sizes,
    tokens,
    order,
    expert_ids,
    norm1_gain,
    w_query,
    w_key,
    w_value,
    w_attn_out,
    rel_table,
    norm2_gain,
    w_router,
    w_in,
    w_out,
    cotangent,
):
    R, D = w_query.shape
    E = w_router.shape[1]
    z = Sizes(*sizes, R, D, E, w_in.shape[2], tokens.shape[1])
    out = layer(
        z,
        tokens.reshape(z.PT, D),
        order,
        expert_ids.reshape(-1, z.PT),
        (norm1_gain, norm2_gain, rel_table),
        (w_query, w_key, w_value, w_attn_out),
        w_router.T,
        w_in,
        w_out,
        cotangent.reshape(z.PT, D),
    )
    g_in, g_out, *rest = expert_weights(
        z, out["slots_ref"], out["hid_ref"], out["gp_ref"], [out[name] for name in PASSED]
    )
    layer_out, gtok, gain1, gq, gk, gv, go, table, gain2, router = rest
    return (
        layer_out.reshape(tokens.shape),
        gtok.reshape(tokens.shape),
        gain1.reshape(R),
        gq,
        gk,
        gv,
        go,
        table.reshape(z.RL),
        gain2.reshape(R),
        router.T,
        g_in,
        g_out,
    )


def solution(mesh):
    everywhere = ("dp", "blk", "head")
    rows, table = P(everywhere), P(everywhere, None)
    tokens = P("dp", ("blk", "head"), None)
    expert = P(("dp", "blk"), None, None)
    in_specs = (
        tokens,
        P("dp", ("blk", "head")),
        P(),
        rows,
        table,
        table,
        table,
        table,
        rows,
        rows,
        table,
        expert,
        expert,
        tokens,
    )
    out_specs = (
        tokens, tokens, rows, table, table, table, table, rows, rows, table, expert, expert
    )
    sizes = (mesh.shape["dp"], mesh.shape["blk"], mesh.shape["head"])
    return jax.shard_map(
        functools.partial(local, sizes),
        mesh=mesh,
        in_specs=in_specs,
        out_specs=out_specs,
        check_vma=False,
    )
```

profile of v0, /device:TPU:0, one launch (start us, length us, event | category | flops | bytes accessed | tf_op | source)
XLA Modules:
  0.0 153.9 jit_solution(11955432531980765972)
XLA Ops:
  0.6 138.6 %layer.1 = (bf16[32,24,3200]{2,1,0:T(8,128)(2,1)}, bf16[2,4,8,24,768]{4,3,2,1,0:T(8,128)(2,1)}, bf16[4,192,3072]{2,1,0:T(8,128)(2,1)}, bf16[4,192,3072]{2,1,0:T(...) custom-call(bf16[128,768]{1,0:T(8,128)(2,1)} %bitcast.13, ...), custom_call_target="tpu_custom_call" | custom-call | tf_op jit(solution)/shard_map/layer/pallas_call | solution.py:1311
  139.3 14.4 %expert_weight_grads.1 = (f32[1,768,3072]{2,1,0:T(8,128)}, f32[1,3072,768]{2,1,0:T(8,128)}, bf16[128,768]{1,0:T(8,128)(2,1)}, bf16[128,768]{1,0:T(8,128)(2,1)}, ...) custom-call(bf16[2,4,8,24,768]{4,3,2,1,0:T(8,128)(2,1)} %get-tuple-e, ...), custom_call_target="tpu_custom_call" | custom-call | tf_op jit(solution)/shard_map/expert_weight_grads/pallas_call | solution.py:1356
where the time goes:
time: 154 us
  Pallas kernels  153 us (99%)
    pallas_call x1, Pallas kernels, layer(): pl.pallas_call(functools.partial(layer_kernel, z, names), out_shape=tuple...  139 us
    pallas_call x1, Pallas kernels, expert_weights(): pl.pallas_call(functools.partial(expert_kernel, z), grid=(z.FF // chunk,)...  14.4 us

commit v1 on v0

--- a/solution.py
+++ b/solution.py
@@ -742,8 +742,9 @@
     probs = exps / jnp.sum(exps, axis=-1, keepdims=True)
     gate = jnp.sum(jnp.where(chosen, probs, 0.0), axis=-1, keepdims=True)
     dispatch(1, (gate * cot).astype(BF16))
-    chunk = D // 2
+    chunk = D
     chunks = z.FF // chunk
+    piece = D // 2
     steps.run_rest(14)
 
     arrivals(0)
@@ -799,12 +800,12 @@
         others_grad = r.act_in[1].astype(F32).reshape(NG * C8, D).astype(BF16)
 
         def step(c, carry):
-            at = pl.ds(pl.multiple_of(c * chunk, chunk), chunk)
+            at = pl.ds(pl.multiple_of(c * piece, piece), piece)
             r.hid[:, at], slope = activate(nn(others_in, r.win[:, at]))
             r.slope[:, at] = grad_pre(others_grad, r.wout[at, :], slope)
             return carry
 
-        lax.fori_loop(0, chunks, step, 0)
+        lax.fori_loop(0, z.FF // piece, step, 0)
         save(hh)
 
     save(h)

time: 154 us -> 152 us (0.987)
  Pallas kernels: 153 us -> 151 us
    pallas_call x1, Pallas kernels: 139 us -> 136 us  [layer(): pl.pallas_call(functools.partial(layer_kernel, z, names), out_shape=tuple...]
where the time goes in v1:
time: 152 us
  Pallas kernels  151 us (99%)
    pallas_call x1, Pallas kernels, layer(): pl.pallas_call(functools.partial(layer_kernel, z, names), out_shape=tuple...  136 us
    pallas_call x1, Pallas kernels, expert_weights(): pl.pallas_call(functools.partial(expert_kernel, z), grid=(z.FF // chunk,)...  14.4 us

profile of v1, /device:TPU:0, one launch (start us, length us, event | category | flops | bytes accessed | tf_op | source)
XLA Modules:
  0.0 151.7 jit_solution(8254570744865040574)
XLA Ops:
  0.6 136.4 %layer.1 = (bf16[32,24,3200]{2,1,0:T(8,128)(2,1)}, bf16[2,4,8,24,768]{4,3,2,1,0:T(8,128)(2,1)}, bf16[4,192,3072]{2,1,0:T(8,128)(2,1)}, bf16[4,192,3072]{2,1,0:T(...) custom-call(bf16[128,768]{1,0:T(8,128)(2,1)} %bitcast.13, ...), custom_call_target="tpu_custom_call" | custom-call | tf_op jit(solution)/shard_map/layer/pallas_call | solution.py:1312
  137.0 14.4 %expert_weight_grads.1 = (f32[1,768,3072]{2,1,0:T(8,128)}, f32[1,3072,768]{2,1,0:T(8,128)}, bf16[128,768]{1,0:T(8,128)(2,1)}, bf16[128,768]{1,0:T(8,128)(2,1)}, ...) custom-call(bf16[2,4,8,24,768]{4,3,2,1,0:T(8,128)(2,1)} %get-tuple-e, ...), custom_call_target="tpu_custom_call" | custom-call | tf_op jit(solution)/shard_map/expert_weight_grads/pallas_call | solution.py:1357
